TPU v7x, 32 devices: a whole 2x2x4 slice. The times are simulated.
32 devices in a mesh: dp: 8 (over z, x), fsdp: 4 (over y, core).
Axes of the slice: x: 2, y: 2, z: 4, core: 2. Of those that a mesh axis runs over, the one named last changes fastest.
Arguments:
- tokens: bfloat16 [16384, 512], P(('dp', 'fsdp')), may hold values from -6 to 6
- lengths: int32 [32], P(('dp', 'fsdp')), may hold values from 256 to 512, as said below
- norm_gains: bfloat16 [2, 2, 512], P(None, None, ('dp', 'fsdp')), may hold values from 0.5 to 1.5
- norm_shifts: bfloat16 [2, 2, 512], P(None, None, ('dp', 'fsdp')), may hold values from -1.796875 to 1.796875
- w_qkv: bfloat16 [2, 512, 1536], P(None, ('dp', 'fsdp')), may hold values from -0.25 to 0.25
- b_qkv: bfloat16 [2, 1536], P(None, ('dp', 'fsdp')), may hold values from -1.796875 to 1.796875
- w_attn: bfloat16 [2, 512, 512], P(None, ('dp', 'fsdp')), may hold values from -2 to 2
- blend_weights: bfloat16 [2, 3, 512], P(None, None, ('dp', 'fsdp')), may hold values from 0.5 to 1.5
- w_in: bfloat16 [2, 512, 2048], P(None, ('dp', 'fsdp')), may hold values from -0.25 to 0.25
- b_in: bfloat16 [2, 2048], P(None, ('dp', 'fsdp')), may hold values from -1.796875 to 1.796875
- w_out: bfloat16 [2, 2048, 512], P(None, ('dp', 'fsdp')), may hold values from -0.125 to 0.125
- out_bias: bfloat16 [2, 2, 512], P(None, None, ('dp', 'fsdp')), may hold values from -1.796875 to 1.796875
- cotangent: bfloat16 [16384, 512], P(('dp', 'fsdp')), may hold values from -6 to 6
Outputs:
- mixed_out: bfloat16 [16384, 512], P(('dp', 'fsdp'))
- grad_tokens: float32 [16384, 512], P(('dp', 'fsdp'))
- grad_norm_gains: float32 [2, 2, 512], P(None, None, ('dp', 'fsdp'))
- grad_norm_shifts: float32 [2, 2, 512], P(None, None, ('dp', 'fsdp'))
- grad_w_qkv: float32 [2, 512, 1536], P(None, ('dp', 'fsdp'))
- grad_b_qkv: float32 [2, 1536], P(None, ('dp', 'fsdp'))
- grad_w_attn: float32 [2, 512, 512], P(None, ('dp', 'fsdp'))
- grad_blend_weights: float32 [2, 3, 512], P(None, None, ('dp', 'fsdp'))
- grad_w_in: float32 [2, 512, 2048], P(None, ('dp', 'fsdp'))
- grad_b_in: float32 [2, 2048], P(None, ('dp', 'fsdp'))
- grad_w_out: float32 [2, 2048, 512], P(None, ('dp', 'fsdp'))
- grad_out_bias: float32 [2, 2, 512], P(None, None, ('dp', 'fsdp'))
Inputs may be any that keep to these rules, and one draw needn't show every extreme that they name: lengths[i] counts the true tokens of the item on device i, rows 0 to lengths[i] - 1 of its 512 rows; some item has exactly 512 and some exactly 256.
All inputs are finite; a program needn't handle non-finite values.
Results may differ from a plain program's by a relative error of at most 0.015.
Values may be sent and summed in bfloat16 or wider, within the bound.
A program may use at most 192 MiB of HBM per device.

v0:
```python
import jax
import jax.numpy as jnp
from jax import lax
from jax.sharding import PartitionSpec as P

HD = 64
BAND = 30
LAYERS = 2


EPSILON = 1e-05
MARGIN = 64
HIGHEST = lax.Precision.HIGHEST


def norm_rows(row_data, gain_row, shift_row):
    centered = row_data - jnp.mean(row_data, axis=-1, keepdims=True)
    variance = jnp.mean(centered * centered, axis=-1, keepdims=True)
    return centered * lax.rsqrt(variance + EPSILON) * gain_row + shift_row


def band_keep(first_row, block_rows, window, length):
    row_pos = first_row + jnp.arange(block_rows, dtype=jnp.int32)
    col_pos = first_row - MARGIN + jnp.arange(window, dtype=jnp.int32)
    offset = col_pos[None, :] - row_pos[:, None]
    inside = (jnp.abs(offset) <= BAND) & (col_pos[None, :] >= 0)
    return inside & ((col_pos[None, :] < length) | (offset == 0))


def pad_rows(values_in):
    return jnp.pad(values_in, ((MARGIN, MARGIN), (0, 0), (0, 0)))


def tile_sizes(seq_rows):
    block_rows = min(512, seq_rows)
    tile_rows = min(128, block_rows)
    return (block_rows, tile_rows, block_rows // tile_rows, tile_rows + 2 * MARGIN)


def tile_windows(padded, first_row, count, tile_rows, window):
    return jnp.stack(
        [
            padded[first_row + n * tile_rows : first_row + n * tile_rows + window]
            for n in range(count)
        ]
    )


def tile_masks(first_row, count, tile_rows, window, length):
    return jnp.stack(
        [band_keep(first_row + n * tile_rows, tile_rows, window, length) for n in range(count)]
    )


def near_forward(queries, keys_in, values_in, length):
    seq_rows, head_count, head_size = queries.shape
    block_rows, tile_rows, count, window = tile_sizes(seq_rows)
    score_scale = head_size ** (-0.5)
    key_pad = pad_rows(keys_in)
    value_pad = pad_rows(values_in)
    key_win = tile_windows(key_pad, 0, count, tile_rows, window)
    value_win = tile_windows(value_pad, 0, count, tile_rows, window)
    query_blk = queries.reshape(count, tile_rows, head_count, head_size)
    scores = (
        jnp.einsum("nqhe,nkhe->nhqk", query_blk, key_win, preferred_element_type=jnp.float32)
        * score_scale
    )
    allowed = tile_masks(0, count, tile_rows, window, length)
    scores = jnp.where(allowed[:, None], scores, -1e30)
    largest = jnp.max(scores, axis=-1, keepdims=True)
    weights = jnp.exp(scores - largest)
    totals = jnp.sum(weights, axis=-1, keepdims=True)
    attention = (weights / totals).astype(jnp.bfloat16)
    result = jnp.einsum("nhqk,nkhe->nqhe", attention, value_win, preferred_element_type=jnp.float32)
    outputs = result.reshape(block_rows, head_count, head_size)
    log_totals = [largest + jnp.log(totals)]
    return (outputs, log_totals)


def near_backward(queries, keys_in, values_in, length, log_totals, grad_mixed_cube, blend_near):
    seq_rows, head_count, head_size = queries.shape
    block_rows, tile_rows, count, window = tile_sizes(seq_rows)
    score_scale = head_size ** (-0.5)
    key_pad = pad_rows(keys_in)
    value_pad = pad_rows(values_in)
    grad_key_pad = jnp.zeros((seq_rows + 2 * MARGIN, head_count, head_size), jnp.float32)
    grad_value_pad = jnp.zeros((seq_rows + 2 * MARGIN, head_count, head_size), jnp.float32)
    grad_query_parts = []
    for block_idx, first_row in enumerate(range(0, seq_rows, block_rows)):
        query_blk = queries.reshape(count, tile_rows, head_count, head_size)
        key_win = tile_windows(key_pad, first_row, count, tile_rows, window)
        value_win = tile_windows(value_pad, first_row, count, tile_rows, window)
        scores = (
            jnp.einsum("nqhe,nkhe->nhqk", query_blk, key_win, preferred_element_type=jnp.float32)
            * score_scale
        )
        allowed = tile_masks(first_row, count, tile_rows, window, length)
        attention = jnp.where(allowed[:, None], jnp.exp(scores - log_totals[block_idx]), 0.0)
        rounded = attention.astype(jnp.bfloat16)
        low_blk = grad_mixed_cube.reshape(count, tile_rows, head_count, head_size)
        grad_blk = low_blk.astype(jnp.float32) * blend_near
        grad_attention = jnp.einsum(
            "nqhe,nkhe->nhqk", grad_blk, value_win.astype(jnp.float32), precision=HIGHEST
        )
        value_terms = (
            jnp.einsum("nhqk,nqhe->nkhe", rounded, low_blk, preferred_element_type=jnp.float32)
            * blend_near
        )
        inner_sum = jnp.sum(attention * grad_attention, axis=-1, keepdims=True)
        grad_scores = attention * (grad_attention - inner_sum) * score_scale
        grad_query = jnp.einsum(
            "nhqk,nkhe->nqhe", grad_scores, key_win.astype(jnp.float32), precision=HIGHEST
        )
        grad_query_parts.append(grad_query.reshape(block_rows, head_count, head_size))
        key_terms = jnp.einsum(
            "nhqk,nqhe->nkhe", grad_scores, query_blk.astype(jnp.float32), precision=HIGHEST
        )
        for tile_idx in range(count):
            low_row = first_row + tile_idx * tile_rows
            grad_value_pad = grad_value_pad.at[low_row : low_row + window].add(
                value_terms[tile_idx]
            )
            grad_key_pad = grad_key_pad.at[low_row : low_row + window].add(key_terms[tile_idx])
    return (
        grad_query_parts[0],
        grad_key_pad[MARGIN : MARGIN + seq_rows],
        grad_value_pad[MARGIN : MARGIN + seq_rows],
    )


def far_forward(queries, keys_in, values_in, keep_cube, length):
    query_full = queries.astype(jnp.float32)
    key_full = keys_in.astype(jnp.float32)
    nothing = jnp.zeros((), jnp.bfloat16)
    phi_query = (jax.nn.elu(query_full) + 1.0).astype(jnp.bfloat16)
    phi_key = jnp.where(keep_cube > 0, (jax.nn.elu(key_full) + 1.0).astype(jnp.bfloat16), nothing)
    state_one = jnp.einsum("khe,khc->hec", phi_key, values_in, preferred_element_type=jnp.float32)
    key_total = jnp.sum(phi_key.astype(jnp.float32), axis=0)
    phi_query_full = phi_query.astype(jnp.float32)
    numerator = jnp.einsum("qhe,hec->qhc", phi_query_full, state_one, precision=HIGHEST)
    denominator = jnp.einsum("qhe,he->qh", phi_query_full, key_total, precision=HIGHEST)[..., None]
    far_elu = numerator / denominator
    tanh_query = jnp.tanh(query_full).astype(jnp.bfloat16)
    tanh_key = jnp.where(keep_cube > 0, jnp.tanh(key_full).astype(jnp.bfloat16), nothing)
    state_two = jnp.einsum("khe,khc->hec", tanh_key, values_in, preferred_element_type=jnp.float32)
    coefficient = lax.rsqrt(queries.shape[2] * length.astype(jnp.float32))
    far_tanh = (
        jnp.einsum("qhe,hec->qhc", tanh_query.astype(jnp.float32), state_two, precision=HIGHEST)
        * coefficient
    )
    far_kept = (
        phi_query,
        phi_key,
        tanh_query,
        tanh_key,
        state_one,
        key_total,
        denominator,
        state_two,
        coefficient,
    )
    return (far_elu, far_tanh, far_kept)


def far_backward(queries, keys_in, values_in, keep_cube, far_kept, far_elu, grad_elu, grad_tanh):
    (
        phi_query,
        phi_key,
        tanh_query,
        tanh_key,
        state_one,
        key_total,
        denominator,
        state_two,
        coefficient,
    ) = far_kept
    query_full = queries.astype(jnp.float32)
    key_full = keys_in.astype(jnp.float32)
    value_full = values_in.astype(jnp.float32)
    phi_query_full = phi_query.astype(jnp.float32)
    grad_numer = grad_elu / denominator
    grad_denom = -jnp.sum(grad_elu * far_elu, axis=-1, keepdims=True) / denominator
    grad_phi_query = (
        jnp.einsum("qhc,hec->qhe", grad_numer, state_one, precision=HIGHEST)
        + grad_denom * key_total[None]
    )
    grad_state_one = jnp.einsum("qhe,qhc->hec", phi_query_full, grad_numer, precision=HIGHEST)
    grad_total = jnp.einsum("qhe,qh->he", phi_query_full, grad_denom[..., 0], precision=HIGHEST)
    grad_phi_key = keep_cube * (
        jnp.einsum("khc,hec->khe", value_full, grad_state_one, precision=HIGHEST) + grad_total[None]
    )
    grad_values = jnp.einsum(
        "khe,hec->khc", phi_key.astype(jnp.float32), grad_state_one, precision=HIGHEST
    )
    scaled_grad = grad_tanh * coefficient
    grad_tanh_query = jnp.einsum("qhc,hec->qhe", scaled_grad, state_two, precision=HIGHEST)
    grad_state_two = jnp.einsum(
        "qhe,qhc->hec", tanh_query.astype(jnp.float32), scaled_grad, precision=HIGHEST
    )
    grad_tanh_key = keep_cube * jnp.einsum(
        "khc,hec->khe", value_full, grad_state_two, precision=HIGHEST
    )
    grad_values = grad_values + jnp.einsum(
        "khe,hec->khc", tanh_key.astype(jnp.float32), grad_state_two, precision=HIGHEST
    )
    slope_query = jnp.where(query_full > 0, 1.0, jnp.exp(query_full))
    slope_key = jnp.where(key_full > 0, 1.0, jnp.exp(key_full))
    tanh_q_full = jnp.tanh(query_full)
    tanh_k_full = jnp.tanh(key_full)
    grad_queries = grad_phi_query * slope_query + grad_tanh_query * (
        1.0 - tanh_q_full * tanh_q_full
    )
    grad_keys = grad_phi_key * slope_key + grad_tanh_key * (1.0 - tanh_k_full * tanh_k_full)
    return (grad_queries, grad_keys, grad_values)


def layer_forward(hidden_in, keep_rows, length, weights):
    (
        gain_rows,
        shift_rows,
        qkv_weight,
        qkv_bias,
        attn_weight,
        blend_rows,
        in_weight,
        in_bias,
        out_weight,
        bias_rows,
    ) = weights
    gain_full = gain_rows.astype(jnp.float32)
    shift_full = shift_rows.astype(jnp.float32)
    blend_full = blend_rows.astype(jnp.float32)
    bias_full = bias_rows.astype(jnp.float32)
    seq_rows = hidden_in.shape[0]
    model_width = attn_weight.shape[0]
    head_count = model_width // HD
    normed = norm_rows(hidden_in, gain_full[0], shift_full[0]).astype(jnp.bfloat16)
    projected = (
        jnp.dot(normed, qkv_weight, preferred_element_type=jnp.float32)
        + qkv_bias.astype(jnp.float32)
    ).astype(jnp.bfloat16)
    queries = projected[:, :model_width].reshape(seq_rows, head_count, HD)
    keys_in = projected[:, model_width : 2 * model_width].reshape(seq_rows, head_count, HD)
    values_in = projected[:, 2 * model_width :].reshape(seq_rows, head_count, HD)
    near_out, log_totals = near_forward(queries, keys_in, values_in, length)
    far_elu, far_tanh, far_kept = far_forward(
        queries, keys_in, values_in, keep_rows[:, :, None], length
    )
    near_flat = near_out.reshape(seq_rows, model_width)
    elu_flat = far_elu.reshape(seq_rows, model_width)
    tanh_flat = far_tanh.reshape(seq_rows, model_width)
    mixed_heads = (
        blend_full[0] * near_flat + blend_full[1] * elu_flat + blend_full[2] * tanh_flat
    ).astype(jnp.bfloat16)
    attn_out = jnp.dot(mixed_heads, attn_weight, preferred_element_type=jnp.float32) + bias_full[0]
    after_attn = hidden_in + keep_rows * attn_out
    normed_two = norm_rows(after_attn, gain_full[1], shift_full[1]).astype(jnp.bfloat16)
    hidden_pre = jnp.dot(
        normed_two, in_weight, preferred_element_type=jnp.float32
    ) + in_bias.astype(jnp.float32)
    activated = jax.nn.gelu(hidden_pre).astype(jnp.bfloat16)
    ffn_out = jnp.dot(activated, out_weight, preferred_element_type=jnp.float32) + bias_full[1]
    layer_out = after_attn + keep_rows * ffn_out
    kept = (
        hidden_in,
        normed,
        queries,
        keys_in,
        values_in,
        log_totals,
        near_flat,
        elu_flat,
        far_elu,
        tanh_flat,
        far_kept,
        mixed_heads,
        after_attn,
        normed_two,
        hidden_pre,
        activated,
    )
    return (layer_out, kept)


def layer_backward(kept, weights, grad_out, keep_rows, length):
    (
        hidden_in,
        normed,
        queries,
        keys_in,
        values_in,
        log_totals,
        near_flat,
        elu_flat,
        far_elu,
        tanh_flat,
        far_kept,
        mixed_heads,
        after_attn,
        normed_two,
        hidden_pre,
        activated,
    ) = kept
    (
        gain_rows,
        shift_rows,
        qkv_weight,
        qkv_bias,
        attn_weight,
        blend_rows,
        in_weight,
        in_bias,
        out_weight,
        bias_rows,
    ) = weights
    gain_full = gain_rows.astype(jnp.float32)
    shift_full = shift_rows.astype(jnp.float32)
    blend_full = blend_rows.astype(jnp.float32)
    seq_rows, head_count, head_size = queries.shape
    model_width = head_count * head_size
    grad_ffn = (keep_rows * grad_out).astype(jnp.bfloat16)
    grad_out_weight = jnp.einsum(
        "tf,td->fd", activated, grad_ffn, preferred_element_type=jnp.float32
    )
    grad_bias_ffn = jnp.sum(grad_ffn.astype(jnp.float32), axis=0)
    grad_act = jnp.einsum("td,fd->tf", grad_ffn, out_weight, preferred_element_type=jnp.float32)
    _, gelu_pull = jax.vjp(jax.nn.gelu, hidden_pre)
    grad_pre = gelu_pull(grad_act)[0].astype(jnp.bfloat16)
    grad_in_weight = jnp.einsum(
        "td,tf->df", normed_two, grad_pre, preferred_element_type=jnp.float32
    )
    grad_in_bias = jnp.sum(grad_pre.astype(jnp.float32), axis=0)
    grad_normed_two = jnp.einsum(
        "tf,df->td", grad_pre, in_weight, preferred_element_type=jnp.float32
    )
    _, second_pull = jax.vjp(norm_rows, after_attn, gain_full[1], shift_full[1])
    grad_after, grad_gain_two, grad_shift_two = second_pull(grad_normed_two)
    grad_after = grad_out + grad_after
    grad_attn = (keep_rows * grad_after).astype(jnp.bfloat16)
    grad_attn_weight = jnp.einsum(
        "tc,td->cd", mixed_heads, grad_attn, preferred_element_type=jnp.float32
    )
    grad_bias_attn = jnp.sum(grad_attn.astype(jnp.float32), axis=0)
    grad_mixed_low = jnp.einsum(
        "td,cd->tc", grad_attn, attn_weight, preferred_element_type=jnp.float32
    ).astype(jnp.bfloat16)
    grad_mixed = grad_mixed_low.astype(jnp.float32)
    grad_blend = jnp.stack(
        [
            jnp.sum(grad_mixed * near_flat, axis=0),
            jnp.sum(grad_mixed * elu_flat, axis=0),
            jnp.sum(grad_mixed * tanh_flat, axis=0),
        ]
    )
    cube_shape = (seq_rows, head_count, head_size)
    grad_q_near, grad_k_near, grad_v_near = near_backward(
        queries,
        keys_in,
        values_in,
        length,
        log_totals,
        grad_mixed_low.reshape(cube_shape),
        blend_full[0].reshape(head_count, head_size),
    )
    grad_q_far, grad_k_far, grad_v_far = far_backward(
        queries,
        keys_in,
        values_in,
        keep_rows[:, :, None],
        far_kept,
        far_elu,
        (blend_full[1] * grad_mixed).reshape(cube_shape),
        (blend_full[2] * grad_mixed).reshape(cube_shape),
    )
    grad_projected = jnp.concatenate(
        [
            (grad_q_near + grad_q_far).reshape(seq_rows, model_width),
            (grad_k_near + grad_k_far).reshape(seq_rows, model_width),
            (grad_v_near + grad_v_far).reshape(seq_rows, model_width),
        ],
        axis=1,
    ).astype(jnp.bfloat16)
    grad_qkv_weight = jnp.einsum(
        "tc,tj->cj", normed, grad_projected, preferred_element_type=jnp.float32
    )
    grad_qkv_bias = jnp.sum(grad_projected.astype(jnp.float32), axis=0)
    grad_normed = jnp.einsum(
        "tj,cj->tc", grad_projected, qkv_weight, preferred_element_type=jnp.float32
    )
    _, first_pull = jax.vjp(norm_rows, hidden_in, gain_full[0], shift_full[0])
    grad_input, grad_gain_one, grad_shift_one = first_pull(grad_normed)
    grad_input = grad_after + grad_input
    gradients = (
        jnp.stack([grad_gain_one, grad_gain_two]),
        jnp.stack([grad_shift_one, grad_shift_two]),
        grad_qkv_weight,
        grad_qkv_bias,
        grad_attn_weight,
        grad_blend,
        grad_in_weight,
        grad_in_bias,
        grad_out_weight,
        jnp.stack([grad_bias_attn, grad_bias_ffn]),
    )
    return (grad_input, gradients)


def on_device(
    tokens,
    lengths,
    norm_gains,
    norm_shifts,
    w_qkv,
    b_qkv,
    w_attn,
    blend_weights,
    w_in,
    b_in,
    w_out,
    out_bias,
    cotangent,
):
    seq_rows = tokens.shape[0]
    length = lengths[0]
    keep_rows = (jnp.arange(seq_rows, dtype=jnp.int32) < length).astype(jnp.float32)[:, None]
    hidden = tokens.astype(jnp.float32)
    fetched = []
    saved = []
    for layer_idx in range(LAYERS):
        weights = (
            lax.all_gather(norm_gains[layer_idx], ("dp", "fsdp"), axis=1, tiled=True),
            lax.all_gather(norm_shifts[layer_idx], ("dp", "fsdp"), axis=1, tiled=True),
            lax.all_gather(w_qkv[layer_idx], ("dp", "fsdp"), axis=0, tiled=True),
            lax.all_gather(b_qkv[layer_idx], ("dp", "fsdp"), axis=0, tiled=True),
            lax.all_gather(w_attn[layer_idx], ("dp", "fsdp"), axis=0, tiled=True),
            lax.all_gather(blend_weights[layer_idx], ("dp", "fsdp"), axis=1, tiled=True),
            lax.all_gather(w_in[layer_idx], ("dp", "fsdp"), axis=0, tiled=True),
            lax.all_gather(b_in[layer_idx], ("dp", "fsdp"), axis=0, tiled=True),
            lax.all_gather(w_out[layer_idx], ("dp", "fsdp"), axis=0, tiled=True),
            lax.all_gather(out_bias[layer_idx], ("dp", "fsdp"), axis=1, tiled=True),
        )
        hidden, kept = layer_forward(hidden, keep_rows, length, weights)
        fetched.append(weights)
        saved.append(kept)
    grad_hidden = cotangent.astype(jnp.float32)
    collected = [None] * LAYERS
    for layer_idx in reversed(range(LAYERS)):
        weights = (
            lax.all_gather(norm_gains[layer_idx], ("dp", "fsdp"), axis=1, tiled=True),
            lax.all_gather(norm_shifts[layer_idx], ("dp", "fsdp"), axis=1, tiled=True),
            lax.all_gather(w_qkv[layer_idx], ("dp", "fsdp"), axis=0, tiled=True),
            lax.all_gather(b_qkv[layer_idx], ("dp", "fsdp"), axis=0, tiled=True),
            lax.all_gather(w_attn[layer_idx], ("dp", "fsdp"), axis=0, tiled=True),
            lax.all_gather(blend_weights[layer_idx], ("dp", "fsdp"), axis=1, tiled=True),
            lax.all_gather(w_in[layer_idx], ("dp", "fsdp"), axis=0, tiled=True),
            lax.all_gather(b_in[layer_idx], ("dp", "fsdp"), axis=0, tiled=True),
            lax.all_gather(w_out[layer_idx], ("dp", "fsdp"), axis=0, tiled=True),
            lax.all_gather(out_bias[layer_idx], ("dp", "fsdp"), axis=1, tiled=True),
        )
        grad_hidden, gradients = layer_backward(
            saved[layer_idx], weights, grad_hidden, keep_rows, length
        )
        collected[layer_idx] = (
            lax.psum_scatter(gradients[0], ("dp", "fsdp"), scatter_dimension=1, tiled=True),
            lax.psum_scatter(gradients[1], ("dp", "fsdp"), scatter_dimension=1, tiled=True),
            lax.psum_scatter(gradients[2], ("dp", "fsdp"), scatter_dimension=0, tiled=True),
            lax.psum_scatter(gradients[3], ("dp", "fsdp"), scatter_dimension=0, tiled=True),
            lax.psum_scatter(gradients[4], ("dp", "fsdp"), scatter_dimension=0, tiled=True),
            lax.psum_scatter(gradients[5], ("dp", "fsdp"), scatter_dimension=1, tiled=True),
            lax.psum_scatter(gradients[6], ("dp", "fsdp"), scatter_dimension=0, tiled=True),
            lax.psum_scatter(gradients[7], ("dp", "fsdp"), scatter_dimension=0, tiled=True),
            lax.psum_scatter(gradients[8], ("dp", "fsdp"), scatter_dimension=0, tiled=True),
            lax.psum_scatter(gradients[9], ("dp", "fsdp"), scatter_dimension=1, tiled=True),
        )
    stacked = tuple(
        (jnp.stack([layer_grads[member] for layer_grads in collected]) for member in range(10))
    )
    return (
        hidden.astype(jnp.bfloat16),
        grad_hidden,
        stacked[0],
        stacked[1],
        stacked[2],
        stacked[3],
        stacked[4],
        stacked[5],
        stacked[6],
        stacked[7],
        stacked[8],
        stacked[9],
    )


def solution(mesh):
    in_specs = (
        P(("dp", "fsdp"), None),
        P(("dp", "fsdp")),
        P(None, None, ("dp", "fsdp")),
        P(None, None, ("dp", "fsdp")),
        P(None, ("dp", "fsdp"), None),
        P(None, ("dp", "fsdp")),
        P(None, ("dp", "fsdp"), None),
        P(None, None, ("dp", "fsdp")),
        P(None, ("dp", "fsdp"), None),
        P(None, ("dp", "fsdp")),
        P(None, ("dp", "fsdp"), None),
        P(None, None, ("dp", "fsdp")),
        P(("dp", "fsdp"), None),
    )
    out_specs = (
        P(("dp", "fsdp"), None),
        P(("dp", "fsdp"), None),
        P(None, None, ("dp", "fsdp")),
        P(None, None, ("dp", "fsdp")),
        P(None, ("dp", "fsdp"), None),
        P(None, ("dp", "fsdp")),
        P(None, ("dp", "fsdp"), None),
        P(None, None, ("dp", "fsdp")),
        P(None, ("dp", "fsdp"), None),
        P(None, ("dp", "fsdp")),
        P(None, ("dp", "fsdp"), None),
        P(None, None, ("dp", "fsdp")),
    )
    return jax.shard_map(
        on_device, mesh=mesh, in_specs=in_specs, out_specs=out_specs, check_vma=False
    )
```

profile of v0, /device:TPU:0, one launch (start us, length us, event | category | flops | bytes accessed | tf_op | source)
XLA Modules:
  0.0 2773.7 jit_solution(3979037512565766116)
XLA Ops:
  19.8 42.2 %all-reduce.17 = (bf16[1536]{0:T(1024)(128)(2,1)S(1)}, bf16[2048]{0:T(1024)(128)(2,1)S(1)}, bf16[1536]{0:T(1024)(128)(2,1)S(1)}, bf16[2048]{0:T(1024)(128)(2,1)S(1)}) all-reduce(bf16[1536]{0:T(1024)(128)(2,1)S(1)} %dynamic-update-slice.48, bf16[2048]{0:T(1024)(128)(2,1)S(1)} %dynamic-update-slice.49, ...), channel_id=6, replica_groups=mesh['dp'=8,'fsdp'=4] {'dp','fsdp'}, use_global_device_ids=true, to_apply=%add.8 | all-reduce | flops 7168 | bytes 28672
  65.3 41.3 %all-gather.1 = bf16[1,2,512]{1,0,2:T(2,128)(2,1)S(1)} all-gather(bf16[1,2,16]{1,0,2:T(2,128)(2,1)S(1)} %copy.298), channel_id=3, replica_groups=mesh['dp'=8,'fsdp'=4] {'dp','fsdp'}, dimensions={2}, use_global_device_ids=true | all-gather | bytes 2112 | tf_op jit(solution)/shard_map/all_gather | solution.py:431
  109.6 37.6 %all-gather.2 = bf16[1,2,512]{1,0,2:T(2,128)(2,1)S(1)} all-gather(bf16[1,2,16]{1,0,2:T(2,128)(2,1)S(1)} %copy.299), channel_id=4, replica_groups=mesh['dp'=8,'fsdp'=4] {'dp','fsdp'}, dimensions={2}, use_global_device_ids=true | all-gather | bytes 2112 | tf_op jit(solution)/shard_map/all_gather | solution.py:432
  150.7 38.7 %all-gather.6 = bf16[1,2,512]{1,0,2:T(2,128)(2,1)S(1)} all-gather(bf16[1,2,16]{1,0,2:T(2,128)(2,1)S(1)} %copy.300), channel_id=8, replica_groups=mesh['dp'=8,'fsdp'=4] {'dp','fsdp'}, dimensions={2}, use_global_device_ids=true | all-gather | bytes 2112 | tf_op jit(solution)/shard_map/all_gather | solution.py:440
  193.1 37.8 %all-gather = bf16[1,3,512]{1,0,2:T(2,128)(2,1)S(1)} all-gather(bf16[1,3,16]{1,0,2:T(2,128)(2,1)S(1)} %copy.297), channel_id=2, replica_groups=mesh['dp'=8,'fsdp'=4] {'dp','fsdp'}, dimensions={2}, use_global_device_ids=true | all-gather | bytes 3168 | tf_op jit(solution)/shard_map/all_gather | solution.py:436
  231.1 5.2 slice_reduce_fusion.17
  237.0 38.5 %all-gather.11 = bf16[1,2,512]{1,0,2:T(2,128)(2,1)S(1)} all-gather(bf16[1,2,16]{1,0,2:T(2,128)(2,1)S(1)} %copy.302), channel_id=13, replica_groups=mesh['dp'=8,'fsdp'=4] {'dp','fsdp'}, dimensions={2}, use_global_device_ids=true | all-gather | bytes 2112 | tf_op jit(solution)/shard_map/all_gather | solution.py:431
  279.1 37.6 %all-gather.12 = bf16[1,2,512]{1,0,2:T(2,128)(2,1)S(1)} all-gather(bf16[1,2,16]{1,0,2:T(2,128)(2,1)S(1)} %copy.303), channel_id=14, replica_groups=mesh['dp'=8,'fsdp'=4] {'dp','fsdp'}, dimensions={2}, use_global_device_ids=true | all-gather | bytes 2112 | tf_op jit(solution)/shard_map/all_gather | solution.py:432
  320.4 39.4 %all-gather.16 = bf16[1,2,512]{1,0,2:T(2,128)(2,1)S(1)} all-gather(bf16[1,2,16]{1,0,2:T(2,128)(2,1)S(1)} %copy.304), channel_id=18, replica_groups=mesh['dp'=8,'fsdp'=4] {'dp','fsdp'}, dimensions={2}, use_global_device_ids=true | all-gather | bytes 2112 | tf_op jit(solution)/shard_map/all_gather | solution.py:440
  363.4 37.4 %all-gather.10 = bf16[1,3,512]{1,0,2:T(2,128)(2,1)S(1)} all-gather(bf16[1,3,16]{1,0,2:T(2,128)(2,1)S(1)} %copy.301), channel_id=12, replica_groups=mesh['dp'=8,'fsdp'=4] {'dp','fsdp'}, dimensions={2}, use_global_device_ids=true | all-gather | bytes 3168 | tf_op jit(solution)/shard_map/all_gather | solution.py:436
  401.1 5.2 slice_reduce_fusion.8
  407.0 42.0 %all-gather.15 = bf16[1,512,512]{2,1,0:T(8,128)(2,1)} all-gather(bf16[1,16,512]{2,1,0:T(8,128)(2,1)S(1)} %get-tuple-element.338), channel_id=17, replica_groups=mesh['dp'=8,'fsdp'=4] {'dp','fsdp'}, dimensions={1}, use_global_device_ids=true | all-gather | bytes 540672 | tf_op jit(solution)/shard_map/all_gather | solution.py:435
  450.5 41.1 %all-gather.5 = bf16[1,512,512]{2,1,0:T(8,128)(2,1)} all-gather(bf16[1,16,512]{2,1,0:T(8,128)(2,1)S(1)} %get-tuple-element.339), channel_id=7, replica_groups=mesh['dp'=8,'fsdp'=4] {'dp','fsdp'}, dimensions={1}, use_global_device_ids=true | all-gather | bytes 540672 | tf_op jit(solution)/shard_map/all_gather | solution.py:435
  521.6 5.0 fusion.38
  526.7 4.9 fusion.356
  566.2 5.0 fusion.30
  571.3 7.5 convert_reduce_fusion
  602.5 4.0 multiply_reduce_fusion.1
  610.4 3.9 convolution_bitcast_fusion.1
  633.2 4.4 convert_reduce_fusion.1
  656.6 4.9 multiply_bitcast_fusion
  661.6 4.0 multiply_reduce_fusion
  665.6 5.7 convolution_bitcast_fusion.4
  671.3 4.3 convolution_bitcast_fusion
  708.9 4.0 fusion.337
  712.9 4.1 fusion.334
  717.4 6.5 fusion.232
  725.0 6.2 fusion.340
  731.9 4.9 fusion.339
  736.9 4.9 fusion.338
  741.9 5.8 fusion.123
  756.3 37.3 %all-reduce.16 = (f32[1536]{0:T(1024)S(1)}, f32[1536]{0:T(1024)S(1)}, f32[2048]{0:T(1024)S(1)}, f32[2048]{0:T(1024)S(1)}) all-reduce(f32[1536]{0:T(1024)S(1)} %convert_reduce_fusion.2, f32[1536]{0:T(1024)S(1)} %convert_reduce_fusion.3, f32[2048]{0:T(1024)S(1)} %copy-done.202, ...), channel_id=29, replica_groups=mesh['dp'=8,'fsdp'=4] {'dp','fsdp'}, use_global_device_ids=true, to_apply=%region_43.44.clone | all-reduce | flops 7168 | bytes 57344
  795.0 12.5 reduce-scatter.55.cloned.1.call-done
  808.3 130.9 %reduce-scatter.63.cloned.1.call-done = f32[16,2]{1,0:T(8,128)} async-done(((f32[512,2]{1,0:T(8,128)}), f32[16,2]{1,0:T(8,128)}) %reduce-scatter.63.cloned.1.call-update) | async-done | bytes 144
  940.0 131.4 %reduce-scatter.51.cloned.1.call-done = f32[16,2]{1,0:T(8,128)} async-done(((f32[512,2]{1,0:T(8,128)}), f32[16,2]{1,0:T(8,128)}) %reduce-scatter.51.cloned.1.call-update) | async-done | bytes 144
  1072.1 130.8 %reduce-scatter.61.cloned.1.call-done = f32[16,2]{1,0:T(8,128)} async-done(((f32[512,2]{1,0:T(8,128)}), f32[16,2]{1,0:T(8,128)}) %reduce-scatter.61.cloned.1.call-update) | async-done | bytes 144
  1203.7 130.8 %reduce-scatter.53.cloned.1.call-done = f32[16,2]{1,0:T(8,128)} async-done(((f32[512,2]{1,0:T(8,128)}), f32[16,2]{1,0:T(8,128)}) %reduce-scatter.53.cloned.1.call-update) | async-done | bytes 144
  1335.3 131.3 %reduce-scatter.49.cloned.1.call-done = f32[16,2]{1,0:T(8,128)} async-done(((f32[512,2]{1,0:T(8,128)}), f32[16,2]{1,0:T(8,128)}) %reduce-scatter.49.cloned.1.call-update) | async-done | bytes 144
  1469.1 129.1 %reduce-scatter.59.cloned.1.call-done = f32[16,3]{1,0:T(8,128)} async-done(((f32[512,3]{1,0:T(8,128)}), f32[16,3]{1,0:T(8,128)}) %reduce-scatter.59.cloned.1.call-update) | async-done | bytes 208
  1599.0 130.8 %reduce-scatter.57.cloned.1.call-done = f32[16,3]{1,0:T(8,128)} async-done(((f32[512,3]{1,0:T(8,128)}), f32[16,3]{1,0:T(8,128)}) %reduce-scatter.57.cloned.1.call-update) | async-done | bytes 208
  1731.1 131.4 %reduce-scatter.39.cloned.1.call-done = f32[16,512]{1,0:T(8,128)} async-done(((f32[512,512]{1,0:T(8,128)}), f32[16,512]{1,0:T(8,128)}) %reduce-scatter.39.cloned.1.call-update) | async-done | bytes 32784 | tf_op jit(solution)/shard_map/reduce_scatter | solution.py:468
  1862.5 132.9 %reduce-scatter.37.cloned.1.call-done = f32[16,512]{1,0:T(8,128)} async-done(((f32[512,512]{1,0:T(8,128)}), f32[16,512]{1,0:T(8,128)}) %reduce-scatter.37.cloned.1.call-update) | async-done | bytes 32784 | tf_op jit(solution)/shard_map/reduce_scatter | solution.py:468
  1996.8 101.3 %reduce-scatter.35.cloned.1.call-done = f32[16,1536]{1,0:T(8,128)} async-done(((f32[512,1536]{1,0:T(8,128)}), f32[16,1536]{1,0:T(8,128)}) %reduce-scatter.35.cloned.1.call-update) | async-done | bytes 98320 | tf_op jit(solution)/shard_map/reduce_scatter | solution.py:466
  2098.1 105.8 %reduce-scatter.33.cloned.1.call-done = f32[16,1536]{1,0:T(8,128)} async-done(((f32[512,1536]{1,0:T(8,128)}), f32[16,1536]{1,0:T(8,128)}) %reduce-scatter.33.cloned.1.call-update) | async-done | bytes 98320 | tf_op jit(solution)/shard_map/reduce_scatter | solution.py:466
  2205.5 141.0 %reduce-scatter.47.cloned.1.call-done = f32[64,512]{1,0:T(8,128)} async-done(((f32[2048,512]{1,0:T(8,128)}), f32[64,512]{1,0:T(8,128)}) %reduce-scatter.47.cloned.1.call-update) | async-done | bytes 131088 | tf_op jit(solution)/shard_map/reduce_scatter | solution.py:472
  2346.5 139.4 %reduce-scatter.45.cloned.1.call-done = f32[64,512]{1,0:T(8,128)} async-done(((f32[2048,512]{1,0:T(8,128)}), f32[64,512]{1,0:T(8,128)}) %reduce-scatter.45.cloned.1.call-update) | async-done | bytes 131088 | tf_op jit(solution)/shard_map/reduce_scatter | solution.py:472
  2487.6 137.6 %reduce-scatter.43.cloned.1.call-done = f32[16,2048]{1,0:T(8,128)} async-done(((f32[512,2048]{1,0:T(8,128)}), f32[16,2048]{1,0:T(8,128)}) %reduce-scatter.43.cloned.1.call-update) | async-done | bytes 131088 | tf_op jit(solution)/shard_map/reduce_scatter | solution.py:470
  2625.2 139.6 %reduce-scatter.41.cloned.1.call-done = f32[16,2048]{1,0:T(8,128)} async-done(((f32[512,2048]{1,0:T(8,128)}), f32[16,2048]{1,0:T(8,128)}) %reduce-scatter.41.cloned.1.call-update) | async-done | bytes 131088 | tf_op jit(solution)/shard_map/reduce_scatter | solution.py:470
  (766 shorter events, 226.9 us)
Async XLA Ops:
  7.2 484.9 %all-gather.27.cloned.1.call-start = ((), (), s32[]{:S(2)}) async-start(), calls=%async_computation.24 | async-start | bytes 1622016 | tf_op jit(solution)/shard_map/all_gather | solution.py:433
  8.7 512.9 %all-gather.29.cloned.1.call-start = ((), (), s32[]{:S(2)}) async-start(), calls=%async_computation.25 | async-start | bytes 2162688 | tf_op jit(solution)/shard_map/all_gather | solution.py:437
  10.3 516.4 %all-gather.31.cloned.1.call-start = ((), (), s32[]{:S(2)}) async-start(), calls=%async_computation.26 | async-start | bytes 2162688 | tf_op jit(solution)/shard_map/all_gather | solution.py:439
  11.9 520.0 %all-gather.33.cloned.1.call-start = ((), (), s32[]{:S(2)}) async-start(), calls=%async_computation.27 | async-start | bytes 1622016 | tf_op jit(solution)/shard_map/all_gather | solution.py:433
  12.5 553.7 %all-gather.35.cloned.1.call-start = ((), (), s32[]{:S(2)}) async-start(), calls=%async_computation.28 | async-start | bytes 2162688 | tf_op jit(solution)/shard_map/all_gather | solution.py:437
  13.1 558.2 %all-gather.37.cloned.1.call-start = ((), (), s32[]{:S(2)}) async-start(), calls=%async_computation.29 | async-start | bytes 2162688 | tf_op jit(solution)/shard_map/all_gather | solution.py:439
  13.7 793.8 %reduce-scatter.55.cloned.1.call-start = ((), (), s32[]{:S(2)}) async-start(), calls=%async_computation.33 | async-start | bytes 270336
  14.5 480.2 %copy-start.185 = (pred[512]{0:T(512)(128)(4,1)}, pred[512]{0:T(512)(128)(4,1)S(1)}, u32[]{:S(2)}) copy-start(pred[512]{0:T(512)(128)(4,1)S(1)} %broadcast_compare_fusion) | copy-start | bytes 1540
  109.6 382.5 %copy-start.145 = (f32[512]{0:T(512)}, f32[512]{0:T(512)S(1)}, u32[]{:S(2)}) copy-start(f32[512]{0:T(512)S(1)} %get-tuple-element.276) | copy-start | bytes 6148
  150.7 341.4 %copy-start.210 = (f32[512]{0:T(512)}, f32[512]{0:T(512)S(1)}, u32[]{:S(2)}) copy-start(f32[512]{0:T(512)S(1)} %get-tuple-element.278) | copy-start | bytes 6148
  189.7 259.2 %copy-start.91 = (bf16[512,512]{1,0:T(8,128)(2,1)S(1)}, bf16[512,512]{1,0:T(8,128)(2,1)}, u32[]{:S(2)}) copy-start(bf16[512,512]{1,0:T(8,128)(2,1)} %param.45) | copy-start | bytes 1572868
  236.4 170.6 %copy-start.155 = (f32[512]{0:T(512)}, f32[512]{0:T(512)S(1)}, u32[]{:S(2)}) copy-start(f32[512]{0:T(512)S(1)} %get-tuple-element.281) | copy-start | bytes 6148
  236.4 283.9 %copy-start.141 = (f32[512]{0:T(512)}, f32[512]{0:T(512)S(1)}, u32[]{:S(2)}) copy-start(f32[512]{0:T(512)S(1)} %get-tuple-element.282) | copy-start | bytes 6148
  236.4 213.1 %copy-start.92 = (bf16[512,512]{1,0:T(8,128)(2,1)S(1)}, bf16[512,512]{1,0:T(8,128)(2,1)}, u32[]{:S(2)}) copy-start(bf16[512,512]{1,0:T(8,128)(2,1)} %param.57) | copy-start | bytes 1572868
  449.1 71.5 %copy-start.9 = (bf16[512,512]{0,1:T(8,128)(2,1)}, bf16[512,512]{0,1:T(8,128)(2,1)S(1)}, u32[]{:S(2)}) copy-start(bf16[512,512]{0,1:T(8,128)(2,1)S(1)} %copy.200) | copy-start | bytes 1572868
  449.3 45.4 %copy-start.136 = (f32[512]{0:T(512)}, f32[512]{0:T(512)S(1)}, u32[]{:S(2)}) copy-start(f32[512]{0:T(512)S(1)} %broadcast_multiply_fusion.3) | copy-start | bytes 6148
  449.5 45.3 %copy-start.161 = (f32[512]{0:T(512)}, f32[512]{0:T(512)S(1)}, u32[]{:S(2)}) copy-start(f32[512]{0:T(512)S(1)} %fusion.144) | copy-start | bytes 6148
  449.5 45.2 %copy-start.157 = (f32[512]{0:T(512)}, f32[512]{0:T(512)S(1)}, u32[]{:S(2)}) copy-start(f32[512]{0:T(512)S(1)} %fusion.281) | copy-start | bytes 6148
  501.1 18.5 copy-start.79
  521.6 10.1 copy-start.163
  521.6 10.1 copy-start.121
  542.3 12.4 copy-start.100
  553.3 9.7 copy-start.4
  565.6 21.1 copy-start.124
  676.5 262.7 %reduce-scatter.63.cloned.1.call-start = ((), (), s32[]{:S(2)}) async-start(), calls=%async_computation.37 | async-start | bytes 270336
  690.8 9.8 copy-start.193
  690.8 10.7 copy-start.179
  690.8 10.7 copy-start.180
  690.8 10.7 copy-start.181
  690.8 11.7 copy-start.182
  690.9 11.7 copy-start.183
  690.9 11.7 copy-start.184
  690.9 12.6 copy-start.46
  697.6 373.8 %reduce-scatter.51.cloned.1.call-start = ((), (), s32[]{:S(2)}) async-start(), calls=%async_computation.31 | async-start | bytes 270336
  698.6 504.3 %reduce-scatter.61.cloned.1.call-start = ((), (), s32[]{:S(2)}) async-start(), calls=%async_computation.36 | async-start | bytes 270336
  699.5 635.0 %reduce-scatter.53.cloned.1.call-start = ((), (), s32[]{:S(2)}) async-start(), calls=%async_computation.32 | async-start | bytes 270336
  699.6 9.2 copy-start.140
  700.5 766.1 %reduce-scatter.49.cloned.1.call-start = ((), (), s32[]{:S(2)}) async-start(), calls=%async_computation.30 | async-start | bytes 270336
  701.5 896.7 %reduce-scatter.59.cloned.1.call-start = ((), (), s32[]{:S(2)}) async-start(), calls=%async_computation.35 | async-start | bytes 270336
  702.5 1027.2 %reduce-scatter.57.cloned.1.call-start = ((), (), s32[]{:S(2)}) async-start(), calls=%async_computation.34 | async-start | bytes 270336
  703.5 1159.1 %reduce-scatter.39.cloned.1.call-start = ((), (), s32[]{:S(2)}) async-start(), calls=%async_computation.19 | async-start | bytes 1081344 | tf_op jit(solution)/shard_map/reduce_scatter | solution.py:468
  706.0 1289.4 %reduce-scatter.37.cloned.1.call-start = ((), (), s32[]{:S(2)}) async-start(), calls=%async_computation.18 | async-start | bytes 1081344 | tf_op jit(solution)/shard_map/reduce_scatter | solution.py:468
  708.8 1389.3 %reduce-scatter.35.cloned.1.call-start = ((), (), s32[]{:S(2)}) async-start(), calls=%async_computation.17 | async-start | bytes 3244032 | tf_op jit(solution)/shard_map/reduce_scatter | solution.py:466
  712.9 1491.0 %reduce-scatter.33.cloned.1.call-start = ((), (), s32[]{:S(2)}) async-start(), calls=%async_computation.16 | async-start | bytes 3244032 | tf_op jit(solution)/shard_map/reduce_scatter | solution.py:466
  717.1 1629.4 %reduce-scatter.47.cloned.1.call-start = ((), (), s32[]{:S(2)}) async-start(), calls=%async_computation.23 | async-start | bytes 4325376 | tf_op jit(solution)/shard_map/reduce_scatter | solution.py:472
  723.9 1762.0 %reduce-scatter.45.cloned.1.call-start = ((), (), s32[]{:S(2)}) async-start(), calls=%async_computation.22 | async-start | bytes 4325376 | tf_op jit(solution)/shard_map/reduce_scatter | solution.py:472
  731.3 1894.0 %reduce-scatter.43.cloned.1.call-start = ((), (), s32[]{:S(2)}) async-start(), calls=%async_computation.21 | async-start | bytes 4325376 | tf_op jit(solution)/shard_map/reduce_scatter | solution.py:470
  736.9 2027.9 %reduce-scatter.41.cloned.1.call-start = ((), (), s32[]{:S(2)}) async-start(), calls=%async_computation.20 | async-start | bytes 4325376 | tf_op jit(solution)/shard_map/reduce_scatter | solution.py:470
  (201 other events, 800.8 us)
Sparse Core Ops, SparseCore 0:
  11.5 58.1 all-gather.26
  72.5 55.8 all-gather.28
  131.9 55.3 all-gather.30
  190.0 53.9 all-gather.32
  246.7 55.7 all-gather.34
  305.7 55.5 all-gather.36
  676.6 130.8 reduce-scatter.54
  809.8 129.3 reduce-scatter.62
  942.0 129.3 reduce-scatter.50
  1073.5 129.3 reduce-scatter.60
  1205.1 129.3 reduce-scatter.52
  1337.2 129.3 reduce-scatter.48
  1468.8 129.3 reduce-scatter.58
  1600.4 129.3 reduce-scatter.56
  1731.8 130.6 reduce-scatter.38
  1864.7 130.6 reduce-scatter.36
  2000.7 97.3 reduce-scatter.34
  2103.4 100.4 reduce-scatter.32
  2206.1 140.3 reduce-scatter.46
  2348.6 137.2 reduce-scatter.44
  2488.2 136.9 reduce-scatter.42
  2627.5 137.2 reduce-scatter.40
where the time goes:
time: 2780 us; the launch traced here: 2770 us
  waiting for transfers between devices  1960 us (71%)
  blocking collectives  471 us (17%)
  matrix products  157 us (6%)
  local copies, waits for them, and re-layouts  112 us (4%)
  other arithmetic  55.6 us (2%)
    unnamed x30, waiting for transfers between devices  929 us
    reduce_scatter x2, waiting for transfers between devices, on_device(): lax.psum_scatter(gradients[8], ('dp', 'fsdp'), scatter_dimension=0, tiled...  280 us
    reduce_scatter x2, waiting for transfers between devices, on_device(): lax.psum_scatter(gradients[6], ('dp', 'fsdp'), scatter_dimension=0, tiled...  277 us
    reduce_scatter x2, waiting for transfers between devices, on_device(): lax.psum_scatter(gradients[4], ('dp', 'fsdp'), scatter_dimension=0, tiled...  264 us
    reduce_scatter x2, waiting for transfers between devices, on_device(): lax.psum_scatter(gradients[2], ('dp', 'fsdp'), scatter_dimension=0, tiled...  207 us
    all_gather x2, blocking collectives, on_device(): lax.all_gather(w_attn[layer_idx], ('dp', 'fsdp'), axis=0, tiled=True)  83.1 us
    all_gather x2, blocking collectives, on_device(): lax.all_gather(norm_gains[layer_idx], ('dp', 'fsdp'), axis=1, tiled=True)  79.8 us
    unnamed x2, blocking collectives  79.5 us
  transfers between devices with their start and end apart: 22, of which 16 were waited for; matrix products, arithmetic and copies ran while one was open for 8% of the time, Pallas kernels for 0%

commit v1 on v0

v1 whole, which is shorter than its diff:
```python
import functools
import itertools
import jax
import jax.numpy as jnp
from jax import lax
from jax.experimental import pallas as pl
from jax.experimental.pallas import tpu as pltpu
from jax.sharding import PartitionSpec as P

HD = 64
BAND = 30
EPSILON = 1e-05
MESH = pl.DeviceIdType.MESH
F32 = jnp.float32
BF16 = jnp.bfloat16
GROUP = 16
TILE = 128
PAD = 32
WINDOW = TILE + 2 * PAD
TWINS = {"acc_t": "acc", "gm_t": "normed"}
ROWS = 64
GELU_C = 0.7978845608028654
GELU_A = 0.044715
GAIN, SHIFT, BQKV, BLEND, BIN, OBIAS, VROWS = 0, 2, 4, 7, 10, 14, 16


def nn(a, b):
    return jnp.dot(a, b, preferred_element_type=F32)


def nt(a, b):
    return lax.dot_general(a, b, (((1,), (1,)), ((), ())), preferred_element_type=F32)


def split(a):
    high = a.astype(BF16)
    return high, (a - high.astype(F32)).astype(BF16)


def row_index(shape):
    return lax.broadcasted_iota(jnp.int32, shape, 0)


def col_index(shape):
    return lax.broadcasted_iota(jnp.int32, shape, 1)


def head_diag(a):
    return jnp.where((row_index(a.shape) < HD) == (col_index(a.shape) < HD), a, 0.0)


def spread(tile):
    top, bottom = tile[:HD], tile[HD:]
    zero = jnp.zeros_like(top)
    return jnp.concatenate(
        [jnp.concatenate([top, zero], axis=1), jnp.concatenate([zero, bottom], axis=1)], axis=0
    )


def fold(wide):
    half = wide.shape[1] // 2
    return jnp.concatenate([wide[:HD, :half], wide[HD:, half:]], axis=0)


def col_sum(a):
    return jnp.sum(a, axis=0, keepdims=True)


GBLEND = 64


def group_shape(width, hidden):
    first = hidden // width
    return (first, width // GROUP // first // 4, 2, 2)


class Net:
    def __init__(self, layers, seq, width, hidden, length, r):
        self.layers, self.seq, self.width, self.hidden = layers, seq, width, hidden
        self.pairs = width // (2 * HD)
        self.tiles = seq // TILE
        self.length = length
        self.padded = seq + TILE
        self.ff_blocks = hidden // width
        self.groups = group_shape(width, hidden)
        self.__dict__.update(r)
        for name, twin in TWINS.items():
            if name not in r:
                setattr(self, name, r[twin])

    @staticmethod
    def scratch(layers, seq, width, hidden):
        padded = seq + TILE
        pairs = width // (2 * HD)
        tiles = seq // TILE
        ff = hidden // width
        v = pltpu.VMEM
        arrays = dict(
            acc=v((seq, width), F32),
            acc_t=v((width, seq), F32),
            xhat=v((layers, 2, seq, width), BF16),
            rstd=v((seq, 128), F32),
            normed=v((seq, width), BF16),
            normed_t=v((layers, 2, width, seq), BF16),
            q_t=v((layers, width, seq), BF16),
            k_pad=v((layers, padded, width), BF16),
            v_pad=v((layers, padded, width), BF16),
            tr_pad=v((width, padded), BF16),
            probs=v((layers, pairs, tiles, WINDOW, 2 * TILE), BF16),
            near_t=v((layers, width, seq), BF16),
            tanh_t=v((layers, width, seq), BF16),
            s_one=v((layers, pairs, 2 * HD, 2 * HD), F32),
            s_two=v((layers, pairs, 2 * HD, 2 * HD), F32),
            rden=v((layers, pairs, 8, seq), F32),
            mixed_t=v((layers, width, seq), BF16),
            act_t=v((layers, ff, width, seq), BF16),
            dact=v((layers, ff, seq, width), BF16),
            band=v((tiles, WINDOW, 2 * TILE), BF16),
            cols=v((width, 128), F32),
            gm_t=v((width, seq), BF16),
            gk_pad=v((padded, width), F32),
            gv_pad=v((padded, width), F32),
            vecs=v((layers, VROWS, width), F32),
            vgrads=v((layers, VROWS, width), F32),
        )
        return {n: a for n, a in arrays.items() if seq != width or n not in TWINS}

    def w_rows(self, l, first):
        return self.packed[l, :, :, :, :, pl.ds(first, GROUP), :].reshape(self.width, self.width)

    def w_qkv(self, l, n):
        return self.w_rows(l, GROUP * n)

    def w_attn(self, l):
        return self.w_rows(l, 3 * GROUP)

    def w_in(self, l, j):
        return self.w_rows(l, pl.multiple_of(4 * GROUP + GROUP * j, GROUP))

    def out_at(self, j):
        per = self.hidden // (self.width // GROUP)
        return j, pl.ds((4 + self.ff_blocks) * GROUP, per)

    def w_out(self, l, j):
        groups, rows = self.out_at(j)
        return self.packed[l, groups, :, :, :, rows, :].reshape(self.width, self.width)

    def put_rows(self, l, first, value):
        self.grads[:, :, :, :, pl.ds(first, GROUP), :] = value.astype(BF16).reshape(
            self.groups + (GROUP, self.width)
        )

    def put_out(self, l, j, value):
        groups, rows = self.out_at(j)
        per = self.hidden // (self.width // GROUP)
        self.grads[groups, :, :, :, rows, :] = value.astype(BF16).reshape(
            self.groups[1:] + (per, self.width)
        )

    def vec(self, l, row):
        return self.vecs[l, pl.ds(row, 1), :]

    def keep(self, value):
        return jnp.where(row_index(value.shape) < self.length, value, 0.0)

    def setup(self):
        shape = (WINDOW, 2 * TILE)
        key, query = row_index(shape) - PAD, col_index(shape) % TILE
        for t in range(self.tiles):
            pos = key + t * TILE
            ok = (jnp.abs(key - query) <= BAND) & (pos >= 0)
            ok = ok & ((pos < self.length) | (key == query))
            self.band[t] = jnp.where(ok, 0.0, -1e30).astype(BF16)
        zero_head = jnp.zeros((PAD, self.width), BF16)
        zero_tail = jnp.zeros((self.padded - PAD - self.seq, self.width), BF16)
        for l in range(self.layers):
            for ref in (self.k_pad, self.v_pad):
                ref[l, :PAD] = zero_head
                ref[l, PAD + self.seq :] = zero_tail

    def setup_vecs(self):
        eye = (row_index((self.width, self.width)) == col_index((self.width, self.width))).astype(
            BF16
        )
        for l in range(self.layers):
            self.cols[:, VROWS * l : VROWS * (l + 1)] = nt(eye, self.vecs[l].astype(BF16))

    def rows(self, body):
        @pl.loop(0, self.seq // ROWS)
        def _(i):
            body(pl.ds(pl.multiple_of(i * ROWS, ROWS), ROWS))

    def norm(self, l, which, source):
        def body(at):
            value = source[at, :]
            centered = value - jnp.mean(value, axis=-1, keepdims=True)
            rstd = lax.rsqrt(jnp.mean(centered * centered, axis=-1, keepdims=True) + EPSILON)
            xhat = centered * rstd
            n = 2 * l + which
            self.rstd[at, n : n + 1] = rstd
            self.xhat[l, which, at, :] = xhat.astype(BF16)
            normed = xhat * self.vec(l, GAIN + which) + self.vec(l, SHIFT + which)
            self.normed[at, :] = normed.astype(BF16)

        self.rows(body)
        self.normed_t[l, which] = self.normed[...].T

    def pad_keep(self):
        row = row_index((self.padded, 2 * HD)) - PAD
        return (row >= 0) & (row < self.length)

    def fwd_qkv(self, l):
        normed = self.normed[...]
        q = (nn(normed, self.w_qkv(l, 0)) + self.vec(l, BQKV)).astype(BF16)
        self.q_t[l] = q.T
        k = (nn(normed, self.w_qkv(l, 1)) + self.vec(l, BQKV + 1)).astype(BF16)
        self.k_pad[l, PAD : PAD + self.seq] = k
        v = (nn(normed, self.w_qkv(l, 2)) + self.vec(l, BQKV + 2)).astype(BF16)
        self.v_pad[l, PAD : PAD + self.seq] = v
        self.tr_pad[...] = self.v_pad[l].T

    def pair_at(self, p):
        return pl.ds(pl.multiple_of(p * 2 * HD, 2 * HD), 2 * HD)

    def fwd_near(self, l, p):
        at = self.pair_at(p)
        for t in range(self.tiles):
            here, window = slice(t * TILE, (t + 1) * TILE), slice(t * TILE, t * TILE + WINDOW)
            wide = spread(self.q_t[l, at, here])
            scores = nn(self.k_pad[l, window, at], wide) * (HD**-0.5) + self.band[t].astype(F32)
            weights = jnp.exp(scores - jnp.max(scores, axis=0, keepdims=True))
            inverse = 1.0 / jnp.sum(weights, axis=0, keepdims=True)
            probs = (weights * inverse).astype(BF16)
            self.probs[l, p, t] = probs
            near = fold(nn(self.tr_pad[at, window], probs))
            self.near_t[l, at, here] = near.astype(BF16)

    def features(self, x):
        grown = jnp.exp(jnp.minimum(x, 0.0))
        return jnp.where(x > 0, x + 1.0, grown), grown, jnp.tanh(x)

    def key_features(self, l, at):
        phi, slope, tanh = self.features(self.k_pad[l, :, at].astype(F32))
        ok = self.pad_keep()
        return (
            jnp.where(ok, phi, 0.0).astype(BF16),
            slope,
            jnp.where(ok, tanh, 0.0).astype(BF16),
            tanh,
        )

    def coefficient(self):
        wide = jnp.full((1, 1), HD, F32) * self.length.astype(F32)
        return lax.rsqrt(wide)

    def heads_row(self, two, seq):
        return jnp.concatenate(
            [
                jnp.broadcast_to(two[0:1], (HD, seq)),
                jnp.broadcast_to(two[1:2], (HD, seq)),
            ],
            axis=0,
        )

    def fwd_far(self, l, p):
        at = self.pair_at(p)
        phk, _, tk, _ = self.key_features(l, at)
        values_t = self.tr_pad[at, :]
        s_one = head_diag(nn(values_t, phk))
        s_two = head_diag(nn(values_t, tk))
        total = col_sum(phk.astype(F32))
        self.s_one[l, p], self.s_two[l, p] = s_one, s_two
        phi, _, tanh = self.features(self.q_t[l, at, :].astype(F32))
        phq, tq = phi.astype(BF16), tanh.astype(BF16)
        shape = (8, 2 * HD)
        mine = (row_index(shape) == 0) == (col_index(shape) < HD)
        z_high, z_low = split(jnp.where(mine & (row_index(shape) < 2), total, 0.0))
        den = nn(z_high, phq) + nn(z_low, phq)
        rden = 1.0 / jnp.where(row_index(den.shape) < 2, den, 1.0)
        self.rden[l, p] = rden
        total_col = jnp.broadcast_to(total, (8, 2 * HD)).T
        n = VROWS * l
        self.cols[at, n : n + 1] = total_col[:, 0:1]
        high, low = split(s_one)
        far_elu = (nn(high, phq) + nn(low, phq)) * self.heads_row(rden, self.seq)
        high, low = split(s_two)
        far_tanh = (nn(high, tq) + nn(low, tq)) * self.coefficient()
        self.tanh_t[l, at, :] = far_tanh.astype(BF16)
        blend = self.cols[at, VROWS * l : VROWS * (l + 1)]
        self.mixed_t[l, at, :] = (
            blend[:, BLEND : BLEND + 1] * self.near_t[l, at, :].astype(F32)
            + blend[:, BLEND + 1 : BLEND + 2] * far_elu
            + blend[:, BLEND + 2 : BLEND + 3] * far_tanh
        ).astype(BF16)

    def fwd_attn(self, l):
        mixed = self.mixed_t[l].T
        out = nn(mixed, self.w_attn(l)) + self.vec(l, OBIAS)
        self.gk_pad[: self.seq] = self.h[...] + self.keep(out)
        self.norm(l, 1, self.gk_pad)

    def fwd_ff(self, l, j):
        pre = nn(self.normed[...], self.w_in(l, j)) + self.vec(l, BIN + j)
        square = pre * pre
        th = jnp.tanh(GELU_C * pre * (1.0 + GELU_A * square))
        half = 0.5 * (1.0 + th)
        act = (pre * half).astype(BF16)
        slope = half + (0.5 * GELU_C) * pre * (1.0 - th * th) * (1.0 + 3.0 * GELU_A * square)
        self.dact[l, j] = slope.astype(BF16)
        self.act_t[l, j] = act.T
        part = nn(act, self.w_out(l, j))
        self.acc[...] = jnp.where(j == 0, part, self.acc[...] + part)

    def fwd_end(self, l):
        self.h[...] = self.gk_pad[: self.seq] + self.keep(self.acc[...] + self.vec(l, OBIAS + 1))

    def put_vec(self, l, row, value):
        self.vgrads[l, pl.ds(row, 1), :] = value

    def bwd_start(self, l):
        gz = self.keep(self.h[...]).astype(BF16)
        self.normed[...] = gz
        self.put_vec(l, OBIAS + 1, col_sum(gz.astype(F32)))

    def bwd_ff(self, l, j):
        gz = self.normed[...]
        gpre = (nt(gz, self.w_out(l, j)) * self.dact[l, j].astype(F32)).astype(BF16)
        self.put_vec(l, BIN + j, col_sum(gpre.astype(F32)))
        self.put_out(l, j, nn(self.act_t[l, j], gz))
        self.put_rows(
            l, pl.multiple_of(4 * GROUP + GROUP * j, GROUP), nn(self.normed_t[l, 1], gpre)
        )
        part = nt(gpre, self.w_in(l, j))
        self.acc[...] = jnp.where(j == 0, part, self.acc[...] + part)

    def norm_back(self, l, which):
        self.put_vec(l, GAIN + which, jnp.zeros((1, self.width), F32))
        self.put_vec(l, SHIFT + which, jnp.zeros((1, self.width), F32))

        def body(at):
            grad = self.acc[at, :]
            xhat = self.xhat[l, which, at, :].astype(F32)
            self.vgrads[l, pl.ds(GAIN + which, 1), :] += col_sum(grad * xhat)
            self.vgrads[l, pl.ds(SHIFT + which, 1), :] += col_sum(grad)
            grad = grad * self.vec(l, GAIN + which)
            mean = jnp.mean(grad, axis=-1, keepdims=True)
            slope = jnp.mean(grad * xhat, axis=-1, keepdims=True)
            n = 2 * l + which
            self.h[at, :] += self.rstd[at, n : n + 1] * (grad - mean - xhat * slope)

        self.rows(body)

    def bwd_attn(self, l):
        self.norm_back(l, 1)
        go = self.keep(self.h[...]).astype(BF16)
        self.put_vec(l, OBIAS, col_sum(go.astype(F32)))
        self.put_rows(l, 3 * GROUP, nn(self.mixed_t[l], go))
        self.gm_t[...] = nt(self.w_attn(l), go).astype(BF16)
        self.tr_pad[...] = self.k_pad[l].T
        self.gk_pad[...] = jnp.zeros_like(self.gk_pad)
        self.gv_pad[...] = jnp.zeros_like(self.gv_pad)

    def bwd_near(self, l, p):
        at = self.pair_at(p)
        blend = self.cols[at, VROWS * l : VROWS * (l + 1)]
        for t in range(self.tiles):
            here, window = slice(t * TILE, (t + 1) * TILE), slice(t * TILE, t * TILE + WINDOW)
            grad = (blend[:, BLEND : BLEND + 1] * self.gm_t[at, here].astype(F32)).astype(BF16)
            grad = spread(grad)
            probs = self.probs[l, p, t]
            wide = probs.astype(F32)
            dprobs = nn(self.v_pad[l, window, at], grad)
            term = wide * dprobs
            inner = jnp.sum(term, axis=0, keepdims=True)
            gs = ((term - wide * inner) * (HD**-0.5)).astype(BF16)
            self.acc_t[at, here] = fold(nn(self.tr_pad[at, window], gs))
            self.gk_pad[window, at] += nt(gs, spread(self.q_t[l, at, here]))
            self.gv_pad[window, at] += nt(probs, grad)

    def bwd_far(self, l, p):
        at = self.pair_at(p)
        seq = self.seq
        blend = self.cols[at, VROWS * l : VROWS * (l + 1)]
        gm = self.gm_t[at, :].astype(F32)
        q = self.q_t[l, at, :].astype(F32)
        phi_q, slope_q, tanh_q = self.features(q)
        phq, tq = phi_q.astype(BF16), tanh_q.astype(BF16)
        high, low = split(self.s_one[l, p])
        far_elu = (nn(high, phq) + nn(low, phq)) * self.heads_row(self.rden[l, p], seq)
        column = lambda a: jnp.sum(a, axis=1, keepdims=True)
        sums = [
            column(gm * self.near_t[l, at, :].astype(F32)),
            column(gm * far_elu),
            column(gm * self.tanh_t[l, at, :].astype(F32)),
        ]
        for n, one in enumerate(sums):
            self.cols[at, GBLEND + n : GBLEND + n + 1] = one
        phk, slope_k, tk, tanh_k = self.key_features(l, at)
        values = self.v_pad[l, :, at]
        gnum = (blend[:, BLEND + 1 : BLEND + 2] * gm * self.heads_row(self.rden[l, p], seq)).astype(
            BF16
        )
        prod = gnum.astype(F32) * far_elu
        gden_one = -col_sum(prod[:HD])
        gden_two = -col_sum(prod[HD:])
        gden = jnp.concatenate([gden_one, gden_two, jnp.zeros((6, seq), F32)], axis=0)
        s_one = self.s_one[l, p].T
        high, low = split(s_one)
        gphq = nn(high, gnum) + nn(low, gnum) + self.cols[at, VROWS * l : VROWS * l + 1] * self.heads_row(gden, seq)
        gs_one = head_diag(nt(phq, gnum))
        gs_high, gs_low = split(gs_one)
        gden_high, gden_low = split(gden)
        both = nt(gden_high, phq) + nt(gden_low, phq)
        gzz = jnp.where(col_index((1, 2 * HD)) < HD, both[0:1], both[1:2])
        gtanh = (blend[:, BLEND + 2 : BLEND + 3] * gm * self.coefficient()).astype(BF16)
        gtq = nn(self.s_two[l, p].T.astype(BF16), gtanh)
        gs_two = head_diag(nt(tq, gtanh)).astype(BF16)
        self.acc_t[at, :] += gphq * jnp.where(q > 0, 1.0, slope_q) + gtq * (1.0 - tanh_q * tanh_q)
        gphk = nt(values, gs_high) + nt(values, gs_low) + gzz
        gtk = nt(values, gs_two)
        grad_k = gphk * slope_k + gtk * (1.0 - tanh_k * tanh_k)
        self.gk_pad[:, at] += jnp.where(self.pad_keep(), grad_k, 0.0)
        self.gv_pad[:, at] += nn(phk, gs_high) + nn(tk, gs_two)

    def bwd_qkv(self, l):
        rows = slice(PAD, PAD + self.seq)
        self.vgrads[l, pl.ds(BLEND, 3), :] = self.cols[...].T[GBLEND : GBLEND + 3]
        normed_t = self.normed_t[l, 0]
        for n in range(3):
            if n == 0:
                grad = self.acc_t[...].T.astype(BF16)
            else:
                grad = (self.gk_pad, self.gv_pad)[n - 1][rows, :].astype(BF16)
            self.put_vec(l, BQKV + n, col_sum(grad.astype(F32)))
            self.put_rows(l, GROUP * n, nn(normed_t, grad))
            part = nt(grad, self.w_qkv(l, n))
            self.acc[...] = part if n == 0 else self.acc[...] + part
        self.norm_back(l, 0)

    def loop(self, count, body):
        @pl.loop(0, count)
        def _(n):
            body(n)


class Comm:
    def __init__(self, depth, sems):
        self.send, self.recv = sems
        self.count = 0
        self.sent = []
        dp, fsdp = lax.axis_index("dp"), lax.axis_index("fsdp")
        self.depth = depth
        self.at = {"z": dp // 2, "x": dp % 2, "y": fsdp // 2, "c": fsdp % 2}

    def device(self, **moved):
        at = dict(self.at, **moved)
        return (at["z"] * 2 + at["x"], at["y"] * 2 + at["c"])

    def other(self, axis, step=1):
        if axis == "z":
            return lax.rem(self.at["z"] + step, self.depth)
        return 1 - self.at[axis]

    def neighbours(self):
        steps = [("z", k) for k in range(1, self.depth)] + [("x", 1), ("y", 1), ("c", 1)]
        return [self.device(**{axis: self.other(axis, k)}) for axis, k in steps]

    def barrier(self):
        semaphore = pltpu.get_barrier_semaphore()
        peers = self.neighbours()
        for peer in peers:
            pl.semaphore_signal(semaphore, inc=1, device_id=peer, device_id_type=MESH)
        pl.semaphore_wait(semaphore, len(peers))

    def copy(self, source, target, peer):
        n = self.count
        self.count += 1
        made = pltpu.make_async_remote_copy(
            src_ref=source,
            dst_ref=target,
            send_sem=self.send.at[n],
            recv_sem=self.recv.at[n],
            device_id=peer,
            device_id_type=MESH,
        )
        made.start()
        return made

    def index(self, whole, moved=None):
        at = dict(self.at, **(moved or {}))
        return tuple(slice(None) if axis in whole else at[axis] for axis in "zxyc")

    @staticmethod
    def add(mine, other):
        @pl.loop(0, mine.shape[0])
        def _(z):
            for rest in itertools.product(*[range(n) for n in mine.shape[1:-2]]):
                at = (z,) + rest
                mine[at] = mine[at] + other[at]

    def gather(self, parts):
        waiting = []
        cores = []
        for stage in range(4):
            started = []
            for view, order in parts:
                whole = order[:stage]
                if stage < 3:
                    axis = order[stage]
                    block = view(self.index(whole))
                    steps = range(1, self.depth) if axis == "z" else (1,)
                    for k in steps:
                        peer = self.device(**{axis: self.other(axis, k)})
                        started.append(self.copy(block, block, peer))
                if stage > 0:
                    axis = order[stage - 1]
                    if axis == "z":
                        block = view(self.index(whole))
                    elif "z" in whole:
                        moved = {axis: self.other(axis)}
                        block = view(self.index(order[: stage - 1], moved))
                    else:
                        continue
                    cores.append(self.copy(block, block, self.device(c=self.other("c"))))
            yield
            for one in started:
                one.wait_recv()
            self.sent += started
        for one in cores:
            one.wait_recv()
        self.sent += cores

    def scatter(self, parts, done):
        pending = []
        stages = ["c"] + [None] * 3
        for stage in range(4):
            started = []
            for view, slots, order in parts:
                axes = ("c",) + tuple(order)
                axis, whole = axes[stage], axes[stage + 1 :]
                if axis == "z":
                    for k in range(1, self.depth):
                        moved = {"z": self.other("z", k)}
                        peer = self.device(**moved)
                        block = view(self.index((), moved))
                        started.append(self.copy(block, slots[stage](k - 1), peer))
                else:
                    moved = {axis: self.other(axis)}
                    block = view(self.index(whole, moved))
                    started.append(self.copy(block, slots[stage](None), self.device(**moved)))
            yield
            for one in started:
                one.wait_recv()
            pending += started
            for view, slots, order in parts:
                axes = ("c",) + tuple(order)
                axis, whole = axes[stage], axes[stage + 1 :]
                if axis != "z":
                    self.add(view(self.index(whole)), slots[stage](None))
                else:
                    total = view(self.index(()))[...].astype(F32)
                    for k in range(1, self.depth):
                        total = total + slots[stage](k - 1)[...].astype(F32)
                    done(view, total)
        for one in pending:
            one.wait_send()


def lane_hits(first, cols, per, lane, rows=128):
    shape = (rows, cols)
    element = col_index(shape) + first
    return (row_index(shape) - lane == element - per * owner_of(element, per)).astype(BF16)


def owner_of(element, per):
    if per & (per - 1) == 0:
        return lax.shift_right_logical(element, per.bit_length() - 1)
    return lax.shift_right_logical(element * (-(-65536 // per)), 16)


def owner_mask(owner, first, cols, per):
    return owner == owner_of(col_index((owner.shape[0], cols)) + first, per)


class Vectors:
    def __init__(self, layers, width, hidden):
        self.layers, self.width = layers, width
        self.devices = width // GROUP
        self.lanes = 128 // layers
        self.wide = [(BQKV, 3, 3 * GROUP), (BIN, hidden // width, hidden // self.devices)]

    def spread(self, shares, vecs):
        width = self.width
        n = self.devices // shares.shape[0]
        vecs[...] = jnp.zeros_like(vecs)

        @pl.loop(0, shares.shape[0])
        def _(z):
            tiles = shares[z].reshape(n, VROWS, 128)
            flat = tiles.reshape(n * VROWS, 128)
            shape = (n * VROWS, width)
            own = owner_mask(n * z + lax.shift_right_logical(row_index(shape), 4), 0, width, GROUP)
            mine = n * z + row_index((n, width))
            for l in range(self.layers):
                lane = self.lanes * l
                rows = nn(flat, lane_hits(0, width, GROUP, lane))
                rows = jnp.sum(jnp.where(own, rows, 0.0).reshape(n, VROWS, width), axis=0)
                for first, last in self.plain_rows():
                    vecs[l, first:last, :] += rows[first:last]
                for row, count, per in self.wide:
                    one = tiles.astype(F32)[:, row, :].astype(BF16)
                    for j in range(count):
                        values = nn(one, lane_hits(j * width, width, per, lane))
                        values = jnp.where(owner_mask(mine, j * width, width, per), values, 0.0)
                        vecs[l, row + j : row + j + 1, :] += col_sum(values)

    def plain_rows(self):
        first, spans = 0, []
        for row, count, _ in self.wide:
            spans.append((first, row))
            first = row + count
        return spans + [(first, VROWS)]

    def collect(self, vgrads, shares):
        width = self.width
        n = self.devices // shares.shape[0]

        def exact(values, hits):
            high, low = split(values)
            return nt(high, hits) + nt(low, hits)

        @pl.loop(0, shares.shape[0])
        def _(z):
            shape = (n * VROWS, width)
            own = owner_mask(n * z + lax.shift_right_logical(row_index(shape), 4), 0, width, GROUP)
            mine = n * z + row_index((n, width))
            result = jnp.zeros((n, VROWS, 128), F32)
            kind = lax.broadcasted_iota(jnp.int32, result.shape, 1)
            for l in range(self.layers):
                lane = self.lanes * l
                rows = vgrads[l]
                wide = jnp.broadcast_to(rows[None], (n, VROWS, width)).reshape(shape)
                part = exact(jnp.where(own, wide, 0.0), lane_hits(0, width, GROUP, lane))
                part = part.reshape(n, VROWS, 128)
                for row, count, per in self.wide:
                    total = jnp.zeros((n, 128), F32)
                    for j in range(count):
                        values = jnp.broadcast_to(rows[row + j : row + j + 1], (n, width))
                        values = jnp.where(owner_mask(mine, j * width, width, per), values, 0.0)
                        total = total + exact(values, lane_hits(j * width, width, per, lane))
                    inside = (kind >= row) & (kind < row + count)
                    first = jnp.broadcast_to(total[:, None, :], part.shape)
                    part = jnp.where(inside, jnp.where(kind == row, first, 0.0), part)
                result = result + part
            shares[z] = result.reshape(shares.shape[1:])


def step(*generators):
    for one in generators:
        next(one, None)


class Program:
    def __init__(self, net, comm, vectors, r):
        self.net, self.comm, self.vectors = net, comm, vectors
        self.__dict__.update(r)

    def fill(self):
        own = self.comm.index(())
        width = self.net.width
        for l in range(self.net.layers):
            first = 0
            for ref in (self.w_qkv, self.w_attn, self.w_in):
                for n in range(ref.shape[2] // width):
                    rows = pl.ds(first, GROUP)
                    self.net.packed[(l,) + own + (rows,)] = ref[l, :, n * width : (n + 1) * width]
                    first += GROUP
            rows = pl.ds(first, self.w_out.shape[1])
            self.net.packed[(l,) + own + (rows,)] = self.w_out[l]
        self.shares[own] = self.small[...]

    def weight_part(self, l, first, rows, order):
        at = pl.ds(first, rows)
        return (lambda index: self.net.packed.at[(l,) + index + (at,)], order)

    def gather(self, l, cuts):
        parts = []
        for first, one, two in cuts:
            parts.append(self.weight_part(l, first, one, "zxy"))
            parts.append(self.weight_part(l, first + one, two, "zyx"))
        if l == 0 and cuts[0][0] == 0:
            parts.append((lambda index: self.shares.at[index], "zxy"))
        return self.comm.gather(parts)

    def scatter(self, l, cuts, vectors=False):
        parts, puts = [], {}

        def add(view, arrivals, at, order, put):
            slots = [
                lambda k: arrivals[0].at[(slice(None),) * 3 + at],
                lambda k: arrivals[1].at[(slice(None),) * 2 + at],
                lambda k: arrivals[2].at[(slice(None),) + at],
                lambda k: arrivals[3].at[(k,) + at],
            ]
            puts[view] = put
            parts.append((view, slots, order))

        def add_rows(first, rows, order):
            at = (pl.ds(first, rows),)
            view = lambda index: self.net.grads.at[index + at]
            add(view, self.arrivals, at, order, functools.partial(self.put, l, first, rows))

        for first, one, two in cuts:
            add_rows(first, one, "yxz")
            add_rows(first + one, two, "xyz")
        if vectors:
            view = lambda index: self.vshares.at[index]
            add(view, self.varrivals, (), "yxz", self.put_small)
        return self.comm.scatter(parts, lambda view, total: puts[view](total))

    def put_small(self, total):
        self.gsmall[...] = total

    def put(self, l, first, rows, total):
        width = self.net.width
        begin = 0
        for ref in (self.gw_qkv, self.gw_attn, self.gw_in):
            for n in range(ref.shape[2] // width):
                if first <= begin < first + rows:
                    ref[l, :, n * width : (n + 1) * width] = total[begin - first :][:GROUP]
                begin += GROUP
        low, high = max(first, begin), first + rows
        if high > low:
            self.gw_out[l, low - begin : high - begin, :] = total[low - first :]

    def run(self):
        net, comm = self.net, self.comm
        loop = net.loop
        cuts = [
            [[(0, 32, 16)], [(48, 32, 48)], [(128, 32, 32)]],
            [[(0, 16, 32)], [(48, 48, 32)], [(128, 32, 32)]],
        ]
        qkv, up, down = zip(*[[self.gather(l, c) for c in cuts[l]] for l in range(2)])
        self.fill()
        comm.barrier()
        step(qkv[0])
        net.setup()
        net.h[...] = self.tokens[...].astype(F32)
        step(qkv[0], up[0], qkv[0], up[0], down[0], qkv[0], qkv[0])
        self.vectors.spread(self.shares, net.vecs)
        net.setup_vecs()
        net.norm(0, 0, net.h)
        net.fwd_qkv(0)
        step(up[0], down[0], qkv[1])
        loop(net.pairs, functools.partial(net.fwd_near, 0))
        step(up[0])
        loop(net.pairs, functools.partial(net.fwd_far, 0))
        step(down[0], qkv[1], up[1], up[0])
        net.fwd_attn(0)
        step(down[0], down[0])
        loop(net.ff_blocks, functools.partial(net.fwd_ff, 0))
        net.fwd_end(0)
        step(qkv[1], up[1], down[1], qkv[1], qkv[1])
        net.norm(1, 0, net.h)
        net.fwd_qkv(1)
        step(up[1], down[1])
        loop(net.pairs, functools.partial(net.fwd_near, 1))
        step(up[1])
        loop(net.pairs, functools.partial(net.fwd_far, 1))
        step(down[1], up[1])
        net.fwd_attn(1)
        step(down[1], down[1])
        loop(net.ff_blocks, functools.partial(net.fwd_ff, 1))
        net.fwd_end(1)
        self.mixed_out[...] = net.h[...].astype(BF16)
        net.h[...] = self.cotangent[...].astype(F32)
        ffs = [self.scatter(l, [(64, 64, 64)]) for l in range(2)]
        rest = [
            self.scatter(0, [(0, 32, 32)], vectors=True),
            self.scatter(1, [(0, 32, 32)]),
        ]
        for l in (1, 0):
            net.bwd_start(l)
            loop(net.ff_blocks, functools.partial(net.bwd_ff, l))
            step(ffs[l])
            if l == 0:
                step(rest[1])
            net.bwd_attn(l)
            step(ffs[l])
            if l == 0:
                step(rest[1])
            loop(net.pairs, functools.partial(net.bwd_near, l))
            step(ffs[l])
            loop(net.pairs, functools.partial(net.bwd_far, l))
            step(ffs[l])
            net.bwd_qkv(l)
            step(ffs[l])
            if l == 0:
                self.vectors.collect(net.vgrads, self.vshares)
            step(rest[l])
            if l == 1:
                step(rest[1], rest[1], rest[1], rest[1])
        step(rest[0], rest[0], rest[0], rest[0])
        for one in comm.sent:
            one.wait_send()


INPUTS = ("tokens", "cotangent", "small", "w_qkv", "w_attn", "w_in", "w_out")
OUTPUTS = ("mixed_out", "h", "gsmall", "gw_qkv", "gw_attn", "gw_in", "gw_out")
COPIES = 160


def fused_body(sizes, depth, names, length_ref, *refs):
    named = dict(zip(INPUTS + OUTPUTS + names, refs))
    arrivals = [named.pop("arrive%d" % n) for n in range(4)]
    varrivals = [named.pop("varrive%d" % n) for n in range(4)]
    sems = named.pop("send"), named.pop("recv")
    inner = {n: r for n, r in named.items() if n not in INPUTS}
    net = Net(*sizes, length_ref[0], inner)
    comm = Comm(depth, sems)
    vectors = Vectors(sizes[0], sizes[2], sizes[3])
    Program(net, comm, vectors, dict(named, arrivals=arrivals, varrivals=varrivals)).run()


def fused(mesh, lengths, tokens, cotangent, small, weights):
    layers, _, width = weights[1].shape
    hidden = weights[2].shape[2]
    seq = tokens.shape[0]
    sizes = (layers, seq, width, hidden)
    rows = sum(w.shape[1] * w.shape[2] for w in weights) // width
    groups = group_shape(width, hidden)
    vmem = pl.BlockSpec(memory_space=pltpu.VMEM)
    scratch = dict(Net.scratch(*sizes))
    scratch["packed"] = pltpu.VMEM((layers,) + groups + (rows, width), BF16)
    scratch["grads"] = pltpu.VMEM(groups + (rows, width), BF16)
    scratch["shares"] = pltpu.VMEM(groups + small.shape, BF16)
    scratch["vshares"] = pltpu.VMEM(groups + small.shape, F32)
    kept = (groups[:3], groups[:2], groups[:1], (groups[0] - 1,))
    for n, lead in enumerate(kept):
        scratch["arrive%d" % n] = pltpu.VMEM(lead + (rows, width), BF16)
        scratch["varrive%d" % n] = pltpu.VMEM(lead + small.shape, F32)
    scratch["send"] = pltpu.SemaphoreType.DMA((COPIES,))
    scratch["recv"] = pltpu.SemaphoreType.DMA((COPIES,))
    return pl.pallas_call(
        functools.partial(fused_body, sizes, groups[0], tuple(scratch)),
        out_shape=(
            jax.ShapeDtypeStruct(tokens.shape, BF16),
            jax.ShapeDtypeStruct(tokens.shape, F32),
            jax.ShapeDtypeStruct(small.shape, F32),
        )
        + tuple(jax.ShapeDtypeStruct(w.shape, F32) for w in weights),
        in_specs=[pl.BlockSpec(memory_space=pltpu.SMEM)] + [vmem] * len(INPUTS),
        out_specs=(vmem,) * len(OUTPUTS),
        scratch_shapes=list(scratch.values()),
        compiler_params=pltpu.CompilerParams(
            collective_id=0, has_side_effects=True, vmem_limit_bytes=63 * 2**20
        ),
    )(lengths, tokens, cotangent, small, *weights)


def pack_small(vectors, layers):
    lanes = 128 // layers
    rows = []
    for v, count in zip(vectors, (2, 2, 3, 3, 4, 2)):
        v = v.reshape(layers, -1, v.shape[-1])
        rows.append(jnp.pad(v, ((0, 0), (0, count - v.shape[1]), (0, lanes - v.shape[2]))))
    return jnp.concatenate(rows, axis=1).transpose(1, 0, 2).reshape(VROWS, 128)


def unpack_small(tile, vectors, layers):
    cube = tile.reshape(VROWS, layers, 128 // layers).transpose(1, 0, 2)
    outs = []
    for v, row in zip(vectors, (GAIN, SHIFT, BQKV, BLEND, BIN, OBIAS)):
        count = 1 if v.ndim == 2 else v.shape[1]
        outs.append(cube[:, row : row + count, : v.shape[-1]].reshape(v.shape))
    return outs


def plain_body(sizes, names, length_ref, *refs):
    names = ("tokens", "cotangent", "packed", "vecs", "mixed_out", "h", "grads_out", "vgrads") + names
    named = dict(zip(names, refs))
    net = Net(*sizes, length_ref[0], named)
    loop = net.loop
    net.setup()
    net.setup_vecs()
    net.h[...] = named["tokens"][...].astype(F32)
    for l in range(net.layers):
        net.norm(l, 0, net.h)
        net.fwd_qkv(l)
        loop(net.pairs, functools.partial(net.fwd_near, l))
        loop(net.pairs, functools.partial(net.fwd_far, l))
        net.fwd_attn(l)
        loop(net.ff_blocks, functools.partial(net.fwd_ff, l))
        net.fwd_end(l)
    named["mixed_out"][...] = net.h[...].astype(BF16)
    net.h[...] = named["cotangent"][...].astype(F32)
    for l in reversed(range(net.layers)):
        net.bwd_start(l)
        loop(net.ff_blocks, functools.partial(net.bwd_ff, l))
        net.bwd_attn(l)
        loop(net.pairs, functools.partial(net.bwd_near, l))
        loop(net.pairs, functools.partial(net.bwd_far, l))
        net.bwd_qkv(l)
        copy = pltpu.make_async_copy(named["grads"], named["grads_out"].at[l], named["sem"])
        copy.start()
        copy.wait()


def plain(lengths, tokens, cotangent, packed, vecs):
    layers, rows, width = packed.shape[0], packed.shape[-2], packed.shape[-1]
    seq = tokens.shape[0]
    hidden = (rows // GROUP - 4) // 2 * width
    sizes = (layers, seq, width, hidden)
    scratch = dict(Net.scratch(*sizes))
    del scratch["vecs"], scratch["vgrads"]
    scratch["grads"] = pltpu.VMEM(packed.shape[1:], BF16)
    scratch["sem"] = pltpu.SemaphoreType.DMA
    vmem = pl.BlockSpec(memory_space=pltpu.VMEM)
    return pl.pallas_call(
        functools.partial(plain_body, sizes, tuple(scratch)),
        out_shape=(
            jax.ShapeDtypeStruct((seq, width), BF16),
            jax.ShapeDtypeStruct((seq, width), F32),
            jax.ShapeDtypeStruct(packed.shape, BF16),
            jax.ShapeDtypeStruct((layers, VROWS, width), F32),
        ),
        in_specs=[pl.BlockSpec(memory_space=pltpu.SMEM)] + [vmem] * 4,
        out_specs=(vmem, vmem, pl.BlockSpec(memory_space=pl.ANY), vmem),
        scratch_shapes=list(scratch.values()),
        compiler_params=pltpu.CompilerParams(vmem_limit_bytes=63 * 2**20),
    )(lengths, tokens, cotangent, packed, vecs)


BOTH = ("dp", "fsdp")


def general(lengths, tokens, cotangent, vectors, weights):
    whole = lambda v, axis: lax.all_gather(v, BOTH, axis=axis, tiled=True)
    w_all = [whole(w, 1) for w in weights]
    v_all = [whole(v, v.ndim - 1) for v in vectors]
    layers, width, _ = w_all[1].shape
    groups = group_shape(width, w_all[2].shape[2])
    blocks = []
    for w in w_all[:3]:
        cut = w.reshape((layers,) + groups + (GROUP, -1, width))
        blocks.append(jnp.moveaxis(cut, -2, -3).reshape((layers,) + groups + (-1, width)))
    blocks.append(w_all[3].reshape((layers,) + groups + (-1, width)))
    vecs = jnp.concatenate([v.reshape(layers, -1, width) for v in v_all], axis=1).astype(F32)
    mixed, grad_tokens, grads, vgrads = plain(
        lengths, tokens, cotangent, jnp.concatenate(blocks, axis=-2), vecs
    )
    reduce = lambda g, axis: lax.psum_scatter(g, BOTH, scatter_dimension=axis, tiled=True)
    w_grads, first = [], 0
    for n, (w, block) in enumerate(zip(w_all, blocks)):
        part = grads[..., first : first + block.shape[-2], :].astype(F32)
        first += block.shape[-2]
        if n < 3:
            part = part.reshape((layers,) + groups + (-1, GROUP, width))
            part = jnp.moveaxis(part, -3, -2)
        w_grads.append(reduce(part.reshape(w.shape), 1))
    v_grads, first = [], 0
    for v in v_all:
        count = v.size // (layers * width)
        part = vgrads[:, first : first + count].reshape(v.shape)
        first += count
        v_grads.append(reduce(part, v.ndim - 1))
    return mixed, grad_tokens, v_grads, w_grads


def on_device(mesh, tokens, lengths, *rest):
    gains, shifts, w_qkv, b_qkv, w_attn, blends, w_in, b_in, w_out, biases, cotangent = rest
    vectors = (gains, shifts, b_qkv, blends, b_in, biases)
    weights = (w_qkv, w_attn, w_in, w_out)
    layers, _, width = w_attn.shape
    groups = group_shape(width, w_in.shape[2])
    if (mesh.shape["dp"], mesh.shape["fsdp"]) == (groups[0] * groups[1], groups[2] * groups[3]):
        small = pack_small(vectors, layers)
        mixed, grad_tokens, tile, *w_grads = fused(
            mesh, lengths, tokens, cotangent, small, weights
        )
        v_grads = unpack_small(tile, vectors, layers)
    else:
        mixed, grad_tokens, v_grads, w_grads = general(
            lengths, tokens, cotangent, vectors, weights
        )
    d_gains, d_shifts, d_b_qkv, d_blends, d_b_in, d_biases = v_grads
    d_w_qkv, d_w_attn, d_w_in, d_w_out = w_grads
    return (
        mixed,
        grad_tokens,
        d_gains,
        d_shifts,
        d_w_qkv,
        d_b_qkv,
        d_w_attn,
        d_blends,
        d_w_in,
        d_b_in,
        d_w_out,
        d_biases,
    )


def solution(mesh):
    rows, vector = P(BOTH, None), P(None, None, BOTH)
    weight, bias = P(None, BOTH, None), P(None, BOTH)
    in_specs = (
        rows,
        P(BOTH),
        vector,
        vector,
        weight,
        bias,
        weight,
        vector,
        weight,
        bias,
        weight,
        vector,
        rows,
    )
    out_specs = (
        rows,
        rows,
        vector,
        vector,
        weight,
        bias,
        weight,
        vector,
        weight,
        bias,
        weight,
        vector,
    )
    return jax.shard_map(
        functools.partial(on_device, mesh),
        mesh=mesh,
        in_specs=in_specs,
        out_specs=out_specs,
        check_vma=False,
    )
```

time: 2780 us -> 252 us (0.09)
  waiting for transfers between devices: 1960 us -> 0 us
  blocking collectives: 471 us -> 0 us
  Pallas kernels: 0 us -> 237 us
  matrix products: 157 us -> 0 us
  local copies, waits for them, and re-layouts: 112 us -> 12.8 us
  other arithmetic: 55.6 us -> 0 us
    reduce_scatter x8 -> x0, waiting for transfers between devices: 1030 us -> none  [the longest x2 280 us: on_device(): lax.psum_scatter(gradients[8], ('dp', 'fsdp'), scatter_dimension=0, tiled...]
    unnamed x30 -> x0, waiting for transfers between devices: 929 us -> none
    all_gather x10 -> x0, blocking collectives: 391 us -> none  [the longest x2 83.1 us: on_device(): lax.all_gather(w_attn[layer_idx], ('dp', 'fsdp'), axis=0, tiled=True)]
    pallas_call x0 -> x1, Pallas kernels: none -> 237 us  [fused(): pl.pallas_call(functools.partial(fused_body, sizes, groups[0], tuple(scra...]
    dot_general x64 -> x0, matrix products: 157 us -> none  [the longest x2 12.8 us: layer_backward(): jnp.einsum('tf,td->fd', activated, grad_ffn, preferred_element_type=jnp.f...]
    unnamed x2 -> x0, blocking collectives: 79.5 us -> none
    slice x30 -> x4, local copies, waits for them, and re-layouts: 50.6 us -> 1.72 us  [unpack_small(): outs.append(cube[:, row:row + count, :v.shape[-1]].reshape(v.shape))]
    reduce_sum x24 -> x0, other arithmetic: 30.2 us -> none  [the longest x6 12 us: norm_rows(): return centered * lax.rsqrt(variance + EPSILON) * gain_row + shift_row]
  transfers between devices with their start and end apart: 22 -> 0, of which waited for: 16 -> 0; matrix products, arithmetic and copies ran while one was open for 8% -> 0% of each run, Pallas kernels for 0% -> 0%
where the time goes in v1:
time: 252 us; the launch traced here: 251 us
  Pallas kernels  237 us (94%)
  local copies, waits for them, and re-layouts  12.8 us (5%)
    pallas_call x1, Pallas kernels, fused(): pl.pallas_call(functools.partial(fused_body, sizes, groups[0], tuple(scra...  237 us
    unnamed x37, local copies, waits for them, and re-layouts  9.53 us

profile of v1, /device:TPU:0, one launch (start us, length us, event | category | flops | bytes accessed | tf_op | source)
XLA Modules:
  0.0 251.4 jit_solution(7005493324976313320)
XLA Ops:
  0.6 0.0 copy-start.6
  1.3 0.0 copy-done.6
  1.3 0.0 copy-start.7
  1.4 0.7 copy-done.7
  2.0 0.0 copy-start.10
  2.0 0.0 copy-start.5
  2.0 0.6 copy-done.10
  2.7 0.0 copy-done.5
  2.7 0.0 copy-start.9
  2.7 0.7 copy-done.9
  3.4 0.0 copy-start.8
  3.4 0.7 copy-done.8
  4.1 0.7 reshape.44.refs_2_
  4.8 237.2 %shard_map.220 = (bf16[512,512]{1,0:T(8,128)(2,1)}, f32[512,512]{1,0:T(8,128)}, f32[16,128]{1,0:T(8,128)}, f32[2,16,1536]{2,1,0:T(8,128)}, f32[2,16,512]{2,1,0:T...) custom-call(s32[1]{0:T(128)S(6)} %copy.43.length_ref, bf16[512,512]{1,0:T(8,128)(2,1)} %refs_0_.1, ...), custom_call_target="tpu_custom_call" | custom-call | tf_op jit(solution)/shard_map/pallas_call | solution.py:844
  242.0 0.0 copy-start
  242.0 0.9 reshape.45
  242.9 0.6 fusion
  243.5 0.6 slice.26
  244.0 0.6 copy.29
  244.6 0.6 slice.28
  245.2 1.9 copy.44
  247.0 0.0 copy-done
  247.0 0.0 copy-start.3
  247.0 1.0 copy.45
  248.0 0.1 copy-done.3
  248.2 0.0 copy-start.4
  248.2 0.0 copy-start.2
  248.2 0.7 copy.46
  248.8 0.2 copy-done.4
  249.0 0.6 copy.47
  249.7 0.0 copy-done.2
  249.7 0.0 copy-start.1
  249.7 0.7 copy.48
  250.4 0.3 copy-done.1
  250.7 0.7 copy.49
  (11 shorter events, 0.1 us)
Async XLA Ops:
  0.6 0.7 copy-start.6
  1.3 0.7 copy-start.7
  2.0 0.7 copy-start.10
  2.0 0.7 copy-start.5
  2.7 0.7 copy-start.9
  3.4 0.7 copy-start.8
  242.0 5.1 %copy-start = (f32[512,512]{1,0:T(8,128)S(1)}, f32[512,512]{1,0:T(8,128)}, u32[]{:S(2)}) copy-start(f32[512,512]{1,0:T(8,128)} %get-tuple-element.54) | copy-start | bytes 3145732
  247.0 1.1 copy-start.3
  248.2 0.9 copy-start.4
  248.2 1.5 copy-start.2
  249.7 1.0 copy-start.1
